TPU v7x, 32 devices: a whole 2x2x4 slice. The times are simulated.
32 devices in a mesh: grp: 2 (over y), seq: 4 (over z), sub: 2 (over x), rep: 2 (over core).
Axes of the slice: x: 2, y: 2, z: 4, core: 2. Of those that a mesh axis runs over, the one named last changes fastest.
Arguments:
- inputs: bfloat16 [16, 4096, 4096], P(('grp', 'rep'), ('seq', 'sub')), parts along dimension 0, may hold values from -6 to 6
- out_grads: bfloat16 [16, 4096, 4096], P(('grp', 'rep'), ('seq', 'sub')), parts along dimension 0, may hold values from -6 to 6
- doc_lengths: int32 [16], P(('grp', 'rep')), parts along dimension 0, may hold values from 512 to 4096, as said below
- in_proj: bfloat16 [4096, 256], replicated, may hold values from -0.09375 to 0.09375
- out_proj: bfloat16 [4096, 256], replicated, may hold values from -0.09375 to 0.09375
- in_factor: float32 [256, 256], replicated, may hold values from -0.25 to 2.25, as said below
- out_factor: float32 [256, 256], replicated, may hold values from -0.25 to 2.25, as said below
- index_rows: bfloat16 [4096, 65536], P('grp', ('seq', 'sub', 'rep')), parts along dimension 0, may hold values from -0.00048828125 to 0.00048828125
Outputs:
- scores: float32 [4096, 8], P(('grp', 'seq', 'sub', 'rep')), parts along dimension 0
There are 2 independent parts, one for each index of `grp`. A program takes and returns all parts, laid end to end along the dimension named above; an argument that names none is the same for every part. Nothing has to cross between parts.
Inputs may be any that keep to these rules, and one draw needn't show every extreme that they name: `doc_lengths`: positions from a document's length on are padding. `in_factor`: symmetric. `out_factor`: symmetric.
All inputs are finite; a program needn't handle non-finite values.
Results may differ from a plain program's by a relative error of at most 0.005.
Values may be sent and summed in bfloat16 or wider, within the bound.
A program may use at most 128 MiB of HBM per device.

v0:
```python
import jax
import jax.numpy as jnp
from jax import lax
from jax.sharding import PartitionSpec as P


def on_device(inputs, out_grads, doc_lengths, in_proj, out_proj, in_factor, out_factor, index_rows):
    doc_count, tok_count, model_width = inputs.shape
    rank_size = in_proj.shape[1]
    offset = lax.axis_index(("seq", "sub")) * tok_count
    positions = offset + jnp.arange(tok_count, dtype=jnp.int32)
    live = positions[None, :] < doc_lengths[:, None]
    in_rows = jnp.dot(
        inputs.reshape(-1, model_width), in_proj, preferred_element_type=jnp.float32
    ).astype(jnp.bfloat16)
    out_rows = jnp.dot(
        out_grads.reshape(-1, model_width), out_proj, preferred_element_type=jnp.float32
    ).astype(jnp.bfloat16)
    factored = jnp.dot(out_rows.astype(jnp.float32), out_factor.T, precision=lax.Precision.HIGHEST)
    factored = factored.reshape(doc_count, tok_count, rank_size) * live[:, :, None].astype(
        jnp.float32
    )
    owned_cols = lax.all_to_all(factored, ("seq", "sub"), split_axis=2, concat_axis=1, tiled=True)
    all_inputs = lax.all_gather(
        in_rows.reshape(doc_count, tok_count, rank_size), ("seq", "sub"), axis=1, tiled=True
    )
    left_grad = jnp.einsum(
        "dto,dti->doi", owned_cols, all_inputs.astype(jnp.float32), precision=lax.Precision.HIGHEST
    )
    owned_block = jnp.einsum("doi,iq->doq", left_grad, in_factor, precision=lax.Precision.HIGHEST)
    owned_sum = owned_block.reshape(doc_count, -1)
    gathered = lax.all_to_all(
        owned_sum.astype(jnp.bfloat16), "rep", split_axis=1, concat_axis=0, tiled=True
    )
    return lax.psum_scatter(
        jnp.dot(index_rows, gathered.T, preferred_element_type=jnp.float32),
        ("seq", "sub", "rep"),
        scatter_dimension=0,
        tiled=True,
    )


def solution(mesh):
    in_specs = (
        P(("grp", "rep"), ("seq", "sub"), None),
        P(("grp", "rep"), ("seq", "sub"), None),
        P(("grp", "rep")),
        P(),
        P(),
        P(),
        P(),
        P("grp", ("seq", "sub", "rep")),
    )
    out_specs = P(("grp", "seq", "sub", "rep"), None)
    return jax.shard_map(
        on_device, mesh=mesh, in_specs=in_specs, out_specs=out_specs, check_vma=False
    )
```

profile of v0, /device:TPU:0, one launch (start us, length us, event | category | flops | bytes accessed | tf_op | source)
XLA Modules:
  0.0 259.7 jit_solution(2755302112089737939)
XLA Ops:
  6.5 0.0 copy-start
  6.5 0.0 all-gather.2.cloned.1.call-start
  6.5 1.6 copy-done
  8.1 9.2 %convolution_convert_fusion = bf16[2048,256]{1,0:T(8,128)(2,1)} fusion(bf16[2048,4096]{1,0:T(8,128)(2,1)} %bitcast.37, bf16[4096,256]{1,0:T(8,128)(2,1)S(1)} %copy-done), kind=kOutput, calls=%fused_computation | convolution fusion | flops 4295491584 | bytes 19922944 | tf_op jit(solution)/shard_map/dot_general | solution.py:13
  17.3 0.0 all-gather.2.cloned.1.call-update
  17.4 0.0 reduce-scatter.2.cloned.1.call-start
  17.4 0.0 copy-start.3
  17.4 11.1 %convolution_convert_fusion.1 = bf16[2048,256]{1,0:T(8,128)(2,1)S(1)} fusion(bf16[2048,4096]{1,0:T(8,128)(2,1)} %bitcast.38, bf16[4096,256]{1,0:T(8,128)(2,1)} %param.12), kind=kOutput, calls=%fused_computation.1 | convolution fusion | flops 4295491584 | bytes 19922944 | tf_op jit(solution)/shard_map/dot_general | solution.py:16
  28.5 2.4 fusion.1
  30.9 2.2 copy.12
  33.2 0.1 compare_convert_fusion
  33.3 0.2 broadcast_multiply_fusion
  33.5 90.6 %all_to_all.34 = f32[4,512,256]{1,0,2:T(4,128)S(1)} all-to-all(f32[4,512,256]{1,0,2:T(4,128)S(1)} %bitcast.30), channel_id=1, replica_groups=mesh['grp'=2,'seq'=4,'sub'=2,'rep'=2] {'seq','sub'}, dimensions={2} | all-to-all | bytes 4194304 | tf_op jit(solution)/shard_map/all_to_all | solution.py:23
  124.2 0.7 copy.13
  124.8 0.2 copy.16
  125.1 55.0 %all-gather.2.cloned.1.call-done = bf16[4,4096,256]{2,1,0:T(8,128)(2,1)} async-done(((bf16[4,512,256]{2,1,0:T(8,128)(2,1)}), bf16[4,4096,256]{2,1,0:T(8,128)(2,1)}) %all-gather.2.cloned.1.call-update) | async-done | bytes 8388624 | tf_op jit(solution)/shard_map/all_gather | solution.py:24
  180.0 6.6 %fusion.2 = f32[4,32,256]{2,1,0:T(8,128)S(1)} fusion(f32[4,4096,32]{1,2,0:T(8,128)S(1)} %bitcast.33, bf16[4,4096,256]{2,1,0:T(8,128)(2,1)} %all-gather.2.cloned.1.call-done), kind=kOutput, calls=%fused_computation.9 | convolution fusion | flops 1610612736 | bytes 10616832 | tf_op jit(solution)/shard_map/dto,dti->doi/dot_general | solution.py:27
  186.6 0.3 convolution_convert_fusion.2
  187.0 0.1 copy.15
  187.0 4.0 %all_to_all.35 = bf16[4,2,4096]{2,0,1:T(4,128)(2,1)S(1)} all-to-all(bf16[4,2,4096]{2,0,1:T(4,128)(2,1)S(1)} %copy.15), channel_id=1, replica_groups=mesh['grp'=2,'seq'=4,'sub'=2,'rep'=2] {'rep'}, dimensions={1} | all-to-all | bytes 131072 | tf_op jit(solution)/shard_map/all_to_all | solution.py:32
  191.0 0.0 copy-start.1
  191.0 11.0 %convolution_bitcast_fusion = f32[2048,8]{0,1:T(8,128)} fusion(bf16[8,4096]{1,0:T(8,128)(2,1)S(1)} %all_to_all.31, bf16[2048,4096]{1,0:T(8,128)(2,1)} %param.15), kind=kOutput, calls=%fused_computation.2 | convolution fusion | flops 134217728 | bytes 16908288 | tf_op jit(solution)/shard_map/dot_general | solution.py:36
  202.0 0.0 reduce-scatter.2.cloned.1.call-update
  202.0 50.8 %reduce-scatter.2.cloned.1.call-done = f32[128,8]{0,1:T(8,128)} async-done(((f32[2048,8]{0,1:T(8,128)}), f32[128,8]{0,1:T(8,128)}) %reduce-scatter.2.cloned.1.call-update) | async-done | bytes 4112 | tf_op jit(solution)/shard_map/reduce_scatter | solution.py:35
  (10 shorter events, 0.1 us)
Async XLA Ops:
  6.5 1.6 copy-start
  6.5 173.5 %all-gather.2.cloned.1.call-start = ((), (), s32[]{:S(2)}) async-start(), calls=%async_computation.3 | async-start | bytes 9437184 | tf_op jit(solution)/shard_map/all_gather | solution.py:24
  17.4 235.5 %reduce-scatter.2.cloned.1.call-start = ((), (), s32[]{:S(2)}) async-start(), calls=%async_computation.4 | async-start | bytes 69632 | tf_op jit(solution)/shard_map/reduce_scatter | solution.py:35
  17.4 11.1 %copy-start.3 = (f32[256,256]{1,0:T(8,128)S(1)}, f32[256,256]{1,0:T(8,128)}, u32[]{:S(2)}) copy-start(f32[256,256]{1,0:T(8,128)} %param.14) | copy-start | bytes 786436
  30.9 2.3 copy-start.4
  180.0 6.6 %copy-start.2 = (f32[256,256]{1,0:T(8,128)S(1)}, f32[256,256]{1,0:T(8,128)}, u32[]{:S(2)}) copy-start(f32[256,256]{1,0:T(8,128)} %param.13) | copy-start | bytes 786436
  191.0 61.8 %copy-start.1 = (bf16[4096,256]{1,0:T(8,128)(2,1)S(1)}, bf16[4096,256]{1,0:T(8,128)(2,1)}, u32[]{:S(2)}) copy-start(bf16[4096,256]{1,0:T(8,128)(2,1)} %param.11) | copy-start | bytes 6291460
Sparse Core Ops, SparseCore 0:
  17.5 162.5 all-gather.1
  202.1 50.6 reduce-scatter.1
where the time goes:
time: 260 us
  waiting for transfers between devices  106 us (41%)
  blocking collectives  94.6 us (36%)
  matrix products  40.5 us (16%)
  between operations  13.5 us (5%)
  local copies, waits for them, and re-layouts  4.85 us (2%)
    all_to_all x1, blocking collectives, on_device(): lax.all_to_all(factored, ('seq', 'sub'), split_axis=2, concat_axis=1, til...  90.6 us
    all_gather x1, waiting for transfers between devices, on_device(): lax.all_gather(in_rows.reshape(doc_count, tok_count, rank_size), ('seq',...  55 us
    reduce_scatter x1, waiting for transfers between devices, on_device(): lax.psum_scatter(jnp.dot(index_rows, gathered.T, preferred_element_type=j...  50.8 us
    dot_general x1, matrix products, on_device(): jnp.dot(out_grads.reshape(-1, model_width), out_proj, preferred_element_t...  11.1 us
    dot_general x1, matrix products, on_device(): jnp.dot(index_rows, gathered.T, preferred_element_type=jnp.float32)  11 us
    dot_general x1, matrix products, on_device(): jnp.dot(inputs.reshape(-1, model_width), in_proj, preferred_element_type=...  9.2 us
    dot_general x1, matrix products, on_device(): jnp.einsum('dto,dti->doi', owned_cols, all_inputs.astype(jnp.float32), pr...  6.57 us
  transfers between devices with their start and end apart: 2, of which 2 were waited for; matrix products, arithmetic and copies ran while one was open for 7% of the time, Pallas kernels for 0%

commit v1 on v0

v1 whole, which is shorter than its diff:
```python
import functools

import jax
import jax.numpy as jnp
from jax import lax
from jax.experimental import pallas as pl
from jax.experimental.pallas import tpu as pltpu
from jax.sharding import PartitionSpec as P

MESH = pl.DeviceIdType.MESH
F32 = jnp.float32
BF16 = jnp.bfloat16
OWNERS = ("seq", "sub", "rep")
PIECES = 4
SLOTS = 8


def two_parts(x):
    high = x.astype(BF16)
    return high, (x - high.astype(F32)).astype(BF16)


def dot3(a, b):
    a_high, a_low = two_parts(a)
    b_high, b_low = two_parts(b)
    small = jnp.dot(a_high, b_low, preferred_element_type=F32) + jnp.dot(
        a_low, b_high, preferred_element_type=F32
    )
    return jnp.dot(a_high, b_high, preferred_element_type=F32) + small


def kernel(
    sizes,
    x_hbm, g_hbm, len_ref, wi_hbm, wo_hbm, fi_hbm, fo_hbm, idx_hbm,
    out_ref,
    xbuf, idxbuf, wi, wo, fi, fo, in_rows, out_rows, send, recv, summed, sc_send, sc_recv,
    piece_sem, idx_sem, weight_sem, send_sem, recv_sem, sc_send_sem, sc_recv_sem,
):
    n_seq, n_sub, n_rep = sizes
    n = n_seq * n_sub * n_rep
    docs, tok, _ = x_hbm.shape
    half = tok // 2
    blocks = n // n_rep
    rows = idx_hbm.shape[0] // blocks
    lanes = rows // n_rep
    place = lax.axis_index("seq") * n_sub + lax.axis_index("sub")
    my_rep = lax.axis_index("rep")
    me = place * n_rep + my_rep

    def device(p):
        return {
            "seq": lax.div(p, n_sub * n_rep),
            "sub": lax.rem(lax.div(p, n_rep), n_sub),
            "rep": lax.rem(p, n_rep),
        }

    def piece_copy(d, q):
        source = x_hbm if q < 2 else g_hbm
        slot = lax.rem(d, SLOTS // PIECES) * PIECES + q
        return pltpu.make_async_copy(
            source.at[d, pl.ds((q % 2) * half, half), :], xbuf.at[slot], piece_sem.at[slot]
        )

    def block_at(t):
        return lax.rem(place + 1 + t, blocks)

    def idx_copy(t):
        c = block_at(t)
        return pltpu.make_async_copy(
            idx_hbm.at[pl.ds(c * rows, rows), :], idxbuf.at[t], idx_sem.at[t]
        )

    def weight_copy(k):
        source, target = ((wi_hbm, wi), (wo_hbm, wo), (fo_hbm, fo), (fi_hbm, fi))[k]
        return pltpu.make_async_copy(source, target, weight_sem.at[k])

    def doc_copy(d, source, p):
        return pltpu.make_async_remote_copy(
            src_ref=send.at[d, p],
            dst_ref=recv.at[source, d],
            send_sem=send_sem.at[d, p],
            recv_sem=recv_sem.at[source, d],
            device_id=device(p),
            device_id_type=MESH,
        )

    def score_copy(source, p):
        return pltpu.make_async_remote_copy(
            src_ref=sc_send.at[p],
            dst_ref=sc_recv.at[source],
            send_sem=sc_send_sem.at[p],
            recv_sem=sc_recv_sem.at[source],
            device_id=device(p),
            device_id_type=MESH,
        )

    weight_copy(0).start()
    piece_copy(0, 0).start()
    piece_copy(0, 1).start()
    weight_copy(1).start()
    piece_copy(0, 2).start()
    piece_copy(0, 3).start()
    weight_copy(2).start()
    weight_copy(3).start()
    for q in range(PIECES):
        piece_copy(1, q).start()

    barrier = pltpu.get_barrier_semaphore()

    def greet(s, carry):
        p = lax.rem(me + s, n)
        pl.semaphore_signal(barrier, inc=1, device_id=device(p), device_id_type=MESH)
        return carry

    lax.fori_loop(1, n, greet, 0)

    def document(d, carry):
        for q in range(PIECES):
            piece_copy(d, q).wait()
            if q % 2 == 0:

                @pl.when(d == 0)
                def _():
                    weight_copy(q // 2).wait()

            slot = lax.rem(d, SLOTS // PIECES) * PIECES + q
            part = pl.ds((q % 2) * half, half)
            w = wi if q < 2 else wo
            product = jnp.dot(xbuf[slot], w[...], preferred_element_type=F32)
            if q < 2:
                in_rows[part, :] = product.astype(BF16)
            else:
                position = (
                    place * tok + (q % 2) * half + lax.broadcasted_iota(jnp.int32, product.shape, 0)
                )
                live = position < len_ref[d]
                out_rows[part, :] = jnp.where(live, product, 0.0).astype(BF16)
            ahead = d + SLOTS // PIECES

            @pl.when(ahead < docs)
            def _():
                piece_copy(ahead, q).start()

            @pl.when(ahead >= docs)
            def _():
                idx_copy((ahead - docs) * PIECES + q).start()

        grad = lax.dot_general(
            out_rows[...], in_rows[...], (((0,), (0,)), ((), ())), preferred_element_type=F32
        )

        @pl.when(d == 0)
        def _():
            weight_copy(2).wait()
            weight_copy(3).wait()

        left = dot3(fo[...], grad)
        send[d] = left.astype(BF16).reshape(send.shape[1:])

        @pl.when(d == 0)
        def _():
            pl.semaphore_wait(barrier, n - 1)

        def push(s, c):
            doc_copy(d, me, lax.rem(me + s, n)).start()
            return c

        lax.fori_loop(1, n, push, 0)
        recv[me, d] = send[d, me]
        return carry

    lax.fori_loop(0, docs, document, 0)

    for d in range(docs):

        def arrive(s, c):
            doc_copy(d, lax.rem(me + n - s, n), lax.rem(me + s, n)).wait_recv()
            return c

        lax.fori_loop(1, n, arrive, 0)
        for r in range(n_rep):
            total = recv[r, d].astype(F32)
            for j in range(1, blocks):
                total = total + recv[j * n_rep + r, d].astype(F32)
            summed[:, r * docs + d, :] = total

    o_rows, all_docs, width = summed.shape
    precond = dot3(summed[...].reshape(o_rows * all_docs, width), fi[...])
    precond = precond.reshape(o_rows, all_docs, width)
    features = jnp.concatenate([precond[o] for o in range(o_rows)], axis=1).astype(BF16)

    def score(t, carry):
        idx_copy(t).wait()
        c = block_at(t)
        part = lax.dot_general(
            features, idxbuf[t], (((1,), (1,)), ((), ())), preferred_element_type=F32
        )
        for r in range(n_rep):
            p = c * n_rep + r
            sc_send[p] = part[:, r * lanes : (r + 1) * lanes]

            @pl.when(p != me)
            def _():
                score_copy(me, p).start()

        return carry

    lax.fori_loop(0, blocks, score, 0)
    sc_recv[me] = sc_send[me]

    def settle(s, carry):
        p = lax.rem(me + s, n)
        score_copy(lax.rem(me + n - s, n), p).wait_recv()
        return carry

    lax.fori_loop(1, n, settle, 0)
    out_ref[...] = jnp.sum(sc_recv[...], axis=0)

    def drain(s, carry):
        p = lax.rem(me + s, n)
        score_copy(me, p).wait_send()
        for d in range(docs):
            doc_copy(d, me, p).wait_send()
        return carry

    lax.fori_loop(1, n, drain, 0)


def fused(sizes, inputs, out_grads, doc_lengths, in_proj, out_proj, in_factor, out_factor, index_rows):
    n = sizes[0] * sizes[1] * sizes[2]
    docs, tok, width = inputs.shape
    rank = in_proj.shape[1]
    rows, features = index_rows.shape
    all_docs = docs * sizes[2]
    o_rows = rank // n
    blocks = n // sizes[2]
    any_ref = pl.BlockSpec(memory_space=pl.ANY)
    scores = pl.pallas_call(
        functools.partial(kernel, sizes),
        out_shape=jax.ShapeDtypeStruct((all_docs, rows // n), F32),
        in_specs=[
            any_ref, any_ref, pl.BlockSpec(memory_space=pltpu.SMEM),
            any_ref, any_ref, any_ref, any_ref, any_ref,
        ],
        out_specs=pl.BlockSpec(memory_space=pltpu.VMEM),
        scratch_shapes=[
            pltpu.VMEM((SLOTS, tok // 2, width), BF16),
            pltpu.VMEM((blocks, rows // blocks, features), BF16),
            pltpu.VMEM(in_proj.shape, BF16),
            pltpu.VMEM(out_proj.shape, BF16),
            pltpu.VMEM(in_factor.shape, F32),
            pltpu.VMEM(out_factor.shape, F32),
            pltpu.VMEM((tok, rank), BF16),
            pltpu.VMEM((tok, rank), BF16),
            pltpu.VMEM((docs, n, o_rows, rank), BF16),
            pltpu.VMEM((n, docs, o_rows, rank), BF16),
            pltpu.VMEM((o_rows, all_docs, rank), F32),
            pltpu.VMEM((n, all_docs, rows // n), F32),
            pltpu.VMEM((n, all_docs, rows // n), F32),
            pltpu.SemaphoreType.DMA((SLOTS,)),
            pltpu.SemaphoreType.DMA((blocks,)),
            pltpu.SemaphoreType.DMA((4,)),
            pltpu.SemaphoreType.DMA((docs, n)),
            pltpu.SemaphoreType.DMA((n, docs)),
            pltpu.SemaphoreType.DMA((n,)),
            pltpu.SemaphoreType.DMA((n,)),
        ],
        compiler_params=pltpu.CompilerParams(
            collective_id=0, has_side_effects=True, vmem_limit_bytes=52 * 1024 * 1024
        ),
    )(inputs, out_grads, doc_lengths, in_proj, out_proj, in_factor, out_factor, index_rows)
    return scores.T


def general(sizes, inputs, out_grads, doc_lengths, in_proj, out_proj, in_factor, out_factor, index_rows):
    docs, tok, width = inputs.shape
    place = lax.axis_index(("seq", "sub"))
    live = place * tok + jnp.arange(tok, dtype=jnp.int32)[None, :] < doc_lengths[:, None]
    in_rows = jnp.einsum("dtk,kr->dtr", inputs, in_proj, preferred_element_type=F32).astype(BF16)
    out_rows = jnp.einsum("dtk,kr->dtr", out_grads, out_proj, preferred_element_type=F32).astype(BF16)
    out_rows = out_rows * live[:, :, None].astype(BF16)
    grad = jnp.einsum("dto,dti->doi", out_rows, in_rows, preferred_element_type=F32)
    left = jnp.einsum("po,doi->dpi", out_factor, grad, precision=lax.Precision.HIGHEST)
    owned = lax.psum_scatter(left, ("seq", "sub"), scatter_dimension=1, tiled=True)
    precond = jnp.einsum("dpi,iq->dpq", owned, in_factor, precision=lax.Precision.HIGHEST)
    precond = precond.reshape(docs, -1).astype(BF16)
    gathered = lax.all_to_all(precond, "rep", split_axis=1, concat_axis=0, tiled=True)
    scores = jnp.dot(index_rows, gathered.T, preferred_element_type=F32)
    return lax.psum_scatter(scores, OWNERS, scatter_dimension=0, tiled=True)


def on_device(sizes, *arrays):
    inputs, in_proj, index_rows = arrays[0], arrays[3], arrays[7]
    n = sizes[0] * sizes[1] * sizes[2]
    docs, tok, width = inputs.shape
    blocks = n // sizes[2]
    whole = (
        in_proj.shape[1] % (16 * n) == 0
        and index_rows.shape[0] % (128 * n) == 0
        and tok % 32 == 0
        and width % 128 == 0
        and (docs * sizes[2]) % 8 == 0
        and docs >= 2
        and blocks == 2 * PIECES
    )
    return (fused if whole else general)(sizes, *arrays)


def solution(mesh):
    in_specs = (
        P(("grp", "rep"), ("seq", "sub"), None),
        P(("grp", "rep"), ("seq", "sub"), None),
        P(("grp", "rep")),
        P(),
        P(),
        P(),
        P(),
        P("grp", OWNERS),
    )
    sizes = tuple(mesh.shape[axis] for axis in OWNERS)
    return jax.shard_map(
        functools.partial(on_device, sizes),
        mesh=mesh,
        in_specs=in_specs,
        out_specs=P(("grp",) + OWNERS, None),
        check_vma=False,
    )
```

time: 260 us -> 46.3 us (0.18)
  waiting for transfers between devices: 106 us -> 0 us
  blocking collectives: 94.6 us -> 0 us
  Pallas kernels: 0 us -> 43 us
  matrix products: 40.5 us -> 0 us
  between operations: 13.5 us -> 0.01 us
    all_to_all x2 -> x0, blocking collectives: 94.6 us -> none  [the longest x1 90.6 us: on_device(): lax.all_to_all(factored, ('seq', 'sub'), split_axis=2, concat_axis=1, til...]
    all_gather x1 -> x0, waiting for transfers between devices: 55 us -> none  [on_device(): lax.all_gather(in_rows.reshape(doc_count, tok_count, rank_size), ('seq',...]
    reduce_scatter x1 -> x0, waiting for transfers between devices: 50.8 us -> none  [on_device(): lax.psum_scatter(jnp.dot(index_rows, gathered.T, preferred_element_type=j...]
    pallas_call x0 -> x1, Pallas kernels: none -> 43 us  [fused(): pl.pallas_call(functools.partial(kernel, sizes), out_shape=jax.ShapeDtype...]
    dot_general x6 -> x0, matrix products: 40.5 us -> none  [the longest x1 11.1 us: on_device(): jnp.dot(out_grads.reshape(-1, model_width), out_proj, preferred_element_t...]
  transfers between devices with their start and end apart: 2 -> 0, of which waited for: 2 -> 0; matrix products, arithmetic and copies ran while one was open for 7% -> 0% of each run, Pallas kernels for 0% -> 0%
where the time goes in v1:
time: 46.3 us; the launch traced here: 46.1 us
  Pallas kernels  43 us (93%)
  local copies, waits for them, and re-layouts  3.15 us (7%)
    pallas_call x1, Pallas kernels, fused(): pl.pallas_call(functools.partial(kernel, sizes), out_shape=jax.ShapeDtype...  43 us
    unnamed x7, local copies, waits for them, and re-layouts  3.15 us

profile of v1, /device:TPU:0, one launch (start us, length us, event | category | flops | bytes accessed | tf_op | source)
XLA Modules:
  0.0 46.1 jit_solution(8400857315952028587)
XLA Ops:
  0.0 0.0 copy-start
  0.0 0.9 %copy-done = f32[256,256]{1,0:T(8,128)S(1)} copy-done((f32[256,256]{1,0:T(8,128)S(1)}, f32[256,256]{1,0:T(8,128)}, u32[]{:S(2)}) %copy-start) | copy-done | bytes 262168
  1.0 0.0 copy-start.1
  1.0 0.9 %copy-done.1 = f32[256,256]{1,0:T(8,128)S(1)} copy-done((f32[256,256]{1,0:T(8,128)S(1)}, f32[256,256]{1,0:T(8,128)}, u32[]{:S(2)}) %copy-start.1) | copy-done | bytes 262168
  1.9 0.0 copy-start.2
  1.9 0.7 %copy-done.2 = s32[4]{0:T(128)S(1)} copy-done((s32[4]{0:T(128)S(1)}, s32[4]{0:T(128)}, u32[]{:S(2)}) %copy-start.2) | copy-done | bytes 40
  2.6 43.0 %shard_map.82 = f32[8,128]{1,0:T(8,128)S(1)} custom-call(bf16[4,512,4096]{2,1,0:T(8,128)(2,1)} %x_hbm.1, bf16[4,512,4096]{2,1,0:T(8,128)(2,1)} %g_hbm.1, s32[4]{0:T(128)S(1)} %copy-done.2, bf16[4096,256]{1,0:T(8,128)(2,1)} %wi_hbm.1, bf16[4096,256]{1,0:T(8,128)(2,1)} %wo_hbm.1, f32[256,256]{1,0:T(8,128)S(1)} %copy-done, f32[256,256]{1,0:T(8,128)S(1)} %copy-done.1, ...), custom_call_target="tpu_custom_call" | custom-call | tf_op jit(solution)/shard_map/pallas_call | solution.py:238
  45.5 0.6 %copy.10 = f32[128,8]{0,1:T(8,128)} copy(f32[128,8]{0,1:T(8,128)S(1)} %bitcast.1) | data formatting | bytes 8192
Async XLA Ops:
  0.0 0.9 %copy-start = (f32[256,256]{1,0:T(8,128)S(1)}, f32[256,256]{1,0:T(8,128)}, u32[]{:S(2)}) copy-start(f32[256,256]{1,0:T(8,128)} %fi_hbm.1) | copy-start | bytes 786436
  1.0 0.9 %copy-start.1 = (f32[256,256]{1,0:T(8,128)S(1)}, f32[256,256]{1,0:T(8,128)}, u32[]{:S(2)}) copy-start(f32[256,256]{1,0:T(8,128)} %fo_hbm.1) | copy-start | bytes 786436
  1.9 0.7 %copy-start.2 = (s32[4]{0:T(128)S(1)}, s32[4]{0:T(128)}, u32[]{:S(2)}) copy-start(s32[4]{0:T(128)} %len_ref.1) | copy-start | bytes 52

commit v2 on v1

--- a/solution.py
+++ b/solution.py
@@ -31,15 +31,15 @@
 
 def kernel(
     sizes,
-    x_hbm, g_hbm, len_ref, wi_hbm, wo_hbm, fi_hbm, fo_hbm, idx_hbm,
+    x_hbm, g_hbm, len_hbm, wi_hbm, wo_hbm, fi_hbm, fo_hbm, idx_hbm,
     out_ref,
-    xbuf, idxbuf, wi, wo, fi, fo, in_rows, out_rows, send, recv, summed, sc_send, sc_recv,
+    xbuf, idxbuf, wi, wo, fi, fo, lens, held, in_rows, out_rows, turned, send, recv, summed, sc_send, sc_recv,
     piece_sem, idx_sem, weight_sem, send_sem, recv_sem, sc_send_sem, sc_recv_sem,
 ):
     n_seq, n_sub, n_rep = sizes
     n = n_seq * n_sub * n_rep
-    docs, tok, _ = x_hbm.shape
-    half = tok // 2
+    docs, tok, width = x_hbm.shape
+    half = width // 2
     blocks = n // n_rep
     rows = idx_hbm.shape[0] // blocks
     lanes = rows // n_rep
@@ -58,7 +58,7 @@
         source = x_hbm if q < 2 else g_hbm
         slot = lax.rem(d, SLOTS // PIECES) * PIECES + q
         return pltpu.make_async_copy(
-            source.at[d, pl.ds((q % 2) * half, half), :], xbuf.at[slot], piece_sem.at[slot]
+            source.at[d, :, pl.ds((q % 2) * half, half)], xbuf.at[slot], piece_sem.at[slot]
         )
 
     def block_at(t):
@@ -71,7 +71,7 @@
         )
 
     def weight_copy(k):
-        source, target = ((wi_hbm, wi), (wo_hbm, wo), (fo_hbm, fo), (fi_hbm, fi))[k]
+        source, target = ((wi_hbm, wi), (wo_hbm, wo), (fo_hbm, fo), (fi_hbm, fi), (len_hbm, lens))[k]
         return pltpu.make_async_copy(source, target, weight_sem.at[k])
 
     def doc_copy(d, source, p):
@@ -102,6 +102,7 @@
     piece_copy(0, 3).start()
     weight_copy(2).start()
     weight_copy(3).start()
+    weight_copy(4).start()
     for q in range(PIECES):
         piece_copy(1, q).start()
 
@@ -122,19 +123,21 @@
                 @pl.when(d == 0)
                 def _():
                     weight_copy(q // 2).wait()
+                    if q == 2:
+                        weight_copy(4).wait()
 
             slot = lax.rem(d, SLOTS // PIECES) * PIECES + q
-            part = pl.ds((q % 2) * half, half)
-            w = wi if q < 2 else wo
-            product = jnp.dot(xbuf[slot], w[...], preferred_element_type=F32)
-            if q < 2:
-                in_rows[part, :] = product.astype(BF16)
+            w = (wi if q < 2 else wo)[(q % 2) * half : (q % 2 + 1) * half, :]
+            product = jnp.dot(xbuf[slot], w, preferred_element_type=F32)
+            if q % 2 == 0:
+                held[...] = product
             else:
-                position = (
-                    place * tok + (q % 2) * half + lax.broadcasted_iota(jnp.int32, product.shape, 0)
-                )
-                live = position < len_ref[d]
-                out_rows[part, :] = jnp.where(live, product, 0.0).astype(BF16)
+                product = held[...] + product
+            if q == 1:
+                in_rows[...] = product.astype(BF16)
+            elif q == 3:
+                position = place * tok + lax.broadcasted_iota(jnp.int32, product.shape, 0)
+                out_rows[...] = jnp.where(position < lens[d], product, 0.0).astype(BF16)
             ahead = d + SLOTS // PIECES
 
             @pl.when(ahead < docs)
@@ -184,28 +187,37 @@
                 total = total + recv[j * n_rep + r, d].astype(F32)
             summed[:, r * docs + d, :] = total
 
-    o_rows, all_docs, width = summed.shape
-    precond = dot3(summed[...].reshape(o_rows * all_docs, width), fi[...])
-    precond = precond.reshape(o_rows, all_docs, width)
-    features = jnp.concatenate([precond[o] for o in range(o_rows)], axis=1).astype(BF16)
-
-    def score(t, carry):
-        idx_copy(t).wait()
-        c = block_at(t)
-        part = lax.dot_general(
-            features, idxbuf[t], (((1,), (1,)), ((), ())), preferred_element_type=F32
-        )
-        for r in range(n_rep):
-            p = c * n_rep + r
-            sc_send[p] = part[:, r * lanes : (r + 1) * lanes]
-
-            @pl.when(p != me)
-            def _():
-                score_copy(me, p).start()
-
-        return carry
-
-    lax.fori_loop(0, blocks, score, 0)
+    o_rows, all_docs, rank = summed.shape
+    columns = o_rows * all_docs
+    precond = dot3(summed[...].reshape(columns, rank), fi[...]).T
+    column = lax.broadcasted_iota(jnp.int32, precond.shape, 1)
+    for o in range(o_rows):
+        mine = (column >= o * all_docs) & (column < (o + 1) * all_docs)
+        turned[o] = jnp.where(mine, precond, 0.0).astype(BF16)
+
+    def score(u, carry):
+        for k in range(n_sub):
+            idx_copy(u * n_sub + k).wait()
+        part = jnp.dot(
+            idxbuf[pl.ds(u * n_sub, n_sub)].reshape(n_sub * rows, o_rows * rank),
+            turned[...].reshape(o_rows * rank, columns),
+            preferred_element_type=F32,
+        ).T
+        part = jnp.sum(part.reshape(o_rows, all_docs, n_sub * rows), axis=0)
+        for k in range(n_sub):
+            c = block_at(u * n_sub + k)
+            for r in range(n_rep):
+                p = c * n_rep + r
+                at = (k * n_rep + r) * lanes
+                sc_send[p] = part[:, at : at + lanes]
+
+                @pl.when(p != me)
+                def _():
+                    score_copy(me, p).start()
+
+        return carry
+
+    lax.fori_loop(0, n_seq, score, 0)
     sc_recv[me] = sc_send[me]
 
     def settle(s, carry):
@@ -234,24 +246,24 @@
     all_docs = docs * sizes[2]
     o_rows = rank // n
     blocks = n // sizes[2]
-    any_ref = pl.BlockSpec(memory_space=pl.ANY)
+    in_hbm = pl.BlockSpec(memory_space=pltpu.HBM)
     scores = pl.pallas_call(
         functools.partial(kernel, sizes),
         out_shape=jax.ShapeDtypeStruct((all_docs, rows // n), F32),
-        in_specs=[
-            any_ref, any_ref, pl.BlockSpec(memory_space=pltpu.SMEM),
-            any_ref, any_ref, any_ref, any_ref, any_ref,
-        ],
+        in_specs=[in_hbm] * 8,
         out_specs=pl.BlockSpec(memory_space=pltpu.VMEM),
         scratch_shapes=[
-            pltpu.VMEM((SLOTS, tok // 2, width), BF16),
+            pltpu.VMEM((SLOTS, tok, width // 2), BF16),
             pltpu.VMEM((blocks, rows // blocks, features), BF16),
             pltpu.VMEM(in_proj.shape, BF16),
             pltpu.VMEM(out_proj.shape, BF16),
             pltpu.VMEM(in_factor.shape, F32),
             pltpu.VMEM(out_factor.shape, F32),
+            pltpu.SMEM((docs,), jnp.int32),
+            pltpu.VMEM((tok, rank), F32),
             pltpu.VMEM((tok, rank), BF16),
             pltpu.VMEM((tok, rank), BF16),
+            pltpu.VMEM((o_rows, rank, o_rows * all_docs), BF16),
             pltpu.VMEM((docs, n, o_rows, rank), BF16),
             pltpu.VMEM((n, docs, o_rows, rank), BF16),
             pltpu.VMEM((o_rows, all_docs, rank), F32),
@@ -259,7 +271,7 @@
             pltpu.VMEM((n, all_docs, rows // n), F32),
             pltpu.SemaphoreType.DMA((SLOTS,)),
             pltpu.SemaphoreType.DMA((blocks,)),
-            pltpu.SemaphoreType.DMA((4,)),
+            pltpu.SemaphoreType.DMA((5,)),
             pltpu.SemaphoreType.DMA((docs, n)),
             pltpu.SemaphoreType.DMA((n, docs)),
             pltpu.SemaphoreType.DMA((n,)),
@@ -297,8 +309,9 @@
     whole = (
         in_proj.shape[1] % (16 * n) == 0
         and index_rows.shape[0] % (128 * n) == 0
-        and tok % 32 == 0
-        and width % 128 == 0
+        and tok % 16 == 0
+        and width % 256 == 0
+        and index_rows.shape[1] == in_proj.shape[1] ** 2 // n
         and (docs * sizes[2]) % 8 == 0
         and docs >= 2
         and blocks == 2 * PIECES

time: 46.3 us -> 45.7 us (0.987)
  Pallas kernels: 43 us -> 42.4 us
    pallas_call x1, Pallas kernels: 43 us -> 42.4 us  [fused(): pl.pallas_call(functools.partial(kernel, sizes), out_shape=jax.ShapeDtype...]
where the time goes in v2:
time: 45.7 us; the launch traced here: 45.5 us
  Pallas kernels  42.4 us (93%)
  local copies, waits for them, and re-layouts  3.15 us (7%)
    pallas_call x1, Pallas kernels, fused(): pl.pallas_call(functools.partial(kernel, sizes), out_shape=jax.ShapeDtype...  42.4 us
    unnamed x7, local copies, waits for them, and re-layouts  3.15 us

profile of v2, /device:TPU:0, one launch (start us, length us, event | category | flops | bytes accessed | tf_op | source)
XLA Modules:
  0.0 45.5 jit_solution(3215045000368509862)
XLA Ops:
  0.0 0.0 copy-start
  0.0 0.9 %copy-done = f32[256,256]{1,0:T(8,128)S(1)} copy-done((f32[256,256]{1,0:T(8,128)S(1)}, f32[256,256]{1,0:T(8,128)}, u32[]{:S(2)}) %copy-start) | copy-done | bytes 262168
  1.0 0.0 copy-start.1
  1.0 0.9 %copy-done.1 = f32[256,256]{1,0:T(8,128)S(1)} copy-done((f32[256,256]{1,0:T(8,128)S(1)}, f32[256,256]{1,0:T(8,128)}, u32[]{:S(2)}) %copy-start.1) | copy-done | bytes 262168
  1.9 0.0 copy-start.2
  1.9 0.7 %copy-done.2 = s32[4]{0:T(128)S(1)} copy-done((s32[4]{0:T(128)S(1)}, s32[4]{0:T(128)}, u32[]{:S(2)}) %copy-start.2) | copy-done | bytes 40
  2.6 42.4 %shard_map.82 = f32[8,128]{1,0:T(8,128)S(1)} custom-call(bf16[4,512,4096]{2,1,0:T(8,128)(2,1)} %x_hbm.1, bf16[4,512,4096]{2,1,0:T(8,128)(2,1)} %g_hbm.1, s32[4]{0:T(128)S(1)} %copy-done.2, bf16[4096,256]{1,0:T(8,128)(2,1)} %wi_hbm.1, bf16[4096,256]{1,0:T(8,128)(2,1)} %wo_hbm.1, f32[256,256]{1,0:T(8,128)S(1)} %copy-done, f32[256,256]{1,0:T(8,128)S(1)} %copy-done.1, ...), custom_call_target="tpu_custom_call" | custom-call | tf_op jit(solution)/shard_map/pallas_call | solution.py:250
  44.9 0.6 %copy.10 = f32[128,8]{0,1:T(8,128)} copy(f32[128,8]{0,1:T(8,128)S(1)} %bitcast.1) | data formatting | bytes 8192
Async XLA Ops:
  0.0 0.9 %copy-start = (f32[256,256]{1,0:T(8,128)S(1)}, f32[256,256]{1,0:T(8,128)}, u32[]{:S(2)}) copy-start(f32[256,256]{1,0:T(8,128)} %fi_hbm.1) | copy-start | bytes 786436
  1.0 0.9 %copy-start.1 = (f32[256,256]{1,0:T(8,128)S(1)}, f32[256,256]{1,0:T(8,128)}, u32[]{:S(2)}) copy-start(f32[256,256]{1,0:T(8,128)} %fo_hbm.1) | copy-start | bytes 786436
  1.9 0.7 %copy-start.2 = (s32[4]{0:T(128)S(1)}, s32[4]{0:T(128)}, u32[]{:S(2)}) copy-start(s32[4]{0:T(128)} %len_hbm.1) | copy-start | bytes 52

commit v3 on v2

--- a/solution.py
+++ b/solution.py
@@ -13,6 +13,13 @@
 OWNERS = ("seq", "sub", "rep")
 PIECES = 4
 SLOTS = 8
+CHAINS = 4
+
+
+def added(parts):
+    while len(parts) > 1:
+        parts = [a + b for a, b in zip(parts[::2], parts[1::2])]
+    return parts[0]
 
 
 def two_parts(x):
@@ -33,13 +40,14 @@
     sizes,
     x_hbm, g_hbm, len_hbm, wi_hbm, wo_hbm, fi_hbm, fo_hbm, idx_hbm,
     out_ref,
-    xbuf, idxbuf, wi, wo, fi, fo, lens, held, in_rows, out_rows, turned, send, recv, summed, sc_send, sc_recv,
+    xbuf, idxbuf, wi, wo, fi, fo, lens, in_rows, out_rows, turned, send, recv, summed, sc_send, sc_recv,
     piece_sem, idx_sem, weight_sem, send_sem, recv_sem, sc_send_sem, sc_recv_sem,
 ):
     n_seq, n_sub, n_rep = sizes
     n = n_seq * n_sub * n_rep
     docs, tok, width = x_hbm.shape
     half = width // 2
+    step = width // CHAINS
     blocks = n // n_rep
     rows = idx_hbm.shape[0] // blocks
     lanes = rows // n_rep
@@ -116,37 +124,44 @@
     lax.fori_loop(1, n, greet, 0)
 
     def document(d, carry):
-        for q in range(PIECES):
+        first = lax.rem(d, SLOTS // PIECES) * PIECES
+        for q in range(0, PIECES, 2):
             piece_copy(d, q).wait()
-            if q % 2 == 0:
-
-                @pl.when(d == 0)
-                def _():
-                    weight_copy(q // 2).wait()
-                    if q == 2:
-                        weight_copy(4).wait()
-
-            slot = lax.rem(d, SLOTS // PIECES) * PIECES + q
-            w = (wi if q < 2 else wo)[(q % 2) * half : (q % 2 + 1) * half, :]
-            product = jnp.dot(xbuf[slot], w, preferred_element_type=F32)
-            if q % 2 == 0:
-                held[...] = product
+            piece_copy(d, q + 1).wait()
+
+            @pl.when(d == 0)
+            def _():
+                weight_copy(q // 2).wait()
+                if q == 2:
+                    weight_copy(4).wait()
+
+            w = wi if q == 0 else wo
+            chains = []
+            for k in range(CHAINS):
+                h, at = (k * 2) // CHAINS, (k % (CHAINS // 2)) * step
+                chains.append(
+                    jnp.dot(
+                        xbuf[first + q + h, :, at : at + step],
+                        w[k * step : (k + 1) * step, :],
+                        preferred_element_type=F32,
+                    )
+                )
+            product = added(chains)
+            if q == 0:
+                in_rows[...] = product.astype(BF16)
             else:
-                product = held[...] + product
-            if q == 1:
-                in_rows[...] = product.astype(BF16)
-            elif q == 3:
                 position = place * tok + lax.broadcasted_iota(jnp.int32, product.shape, 0)
                 out_rows[...] = jnp.where(position < lens[d], product, 0.0).astype(BF16)
             ahead = d + SLOTS // PIECES
-
-            @pl.when(ahead < docs)
-            def _():
-                piece_copy(ahead, q).start()
-
-            @pl.when(ahead >= docs)
-            def _():
-                idx_copy((ahead - docs) * PIECES + q).start()
+            for k in (q, q + 1):
+
+                @pl.when(ahead < docs)
+                def _():
+                    piece_copy(ahead, k).start()
+
+                @pl.when(ahead >= docs)
+                def _():
+                    idx_copy((ahead - docs) * PIECES + k).start()
 
         grad = lax.dot_general(
             out_rows[...], in_rows[...], (((0,), (0,)), ((), ())), preferred_element_type=F32
@@ -198,11 +213,18 @@
     def score(u, carry):
         for k in range(n_sub):
             idx_copy(u * n_sub + k).wait()
-        part = jnp.dot(
-            idxbuf[pl.ds(u * n_sub, n_sub)].reshape(n_sub * rows, o_rows * rank),
-            turned[...].reshape(o_rows * rank, columns),
-            preferred_element_type=F32,
-        ).T
+        parts = []
+        for k in range(CHAINS):
+            o, wide = k * (o_rows // CHAINS), o_rows // CHAINS
+            block = idxbuf[pl.ds(u * n_sub, n_sub), :, o * rank : (o + wide) * rank]
+            parts.append(
+                jnp.dot(
+                    block.reshape(n_sub * rows, wide * rank),
+                    turned[o : o + wide].reshape(wide * rank, columns),
+                    preferred_element_type=F32,
+                )
+            )
+        part = added(parts).T
         part = jnp.sum(part.reshape(o_rows, all_docs, n_sub * rows), axis=0)
         for k in range(n_sub):
             c = block_at(u * n_sub + k)
@@ -260,7 +282,6 @@
             pltpu.VMEM(in_factor.shape, F32),
             pltpu.VMEM(out_factor.shape, F32),
             pltpu.SMEM((docs,), jnp.int32),
-            pltpu.VMEM((tok, rank), F32),
             pltpu.VMEM((tok, rank), BF16),
             pltpu.VMEM((tok, rank), BF16),
             pltpu.VMEM((o_rows, rank, o_rows * all_docs), BF16),
@@ -278,7 +299,7 @@
             pltpu.SemaphoreType.DMA((n,)),
         ],
         compiler_params=pltpu.CompilerParams(
-            collective_id=0, has_side_effects=True, vmem_limit_bytes=52 * 1024 * 1024
+            collective_id=0, has_side_effects=True, vmem_limit_bytes=64 * 1024 * 1024
         ),
     )(inputs, out_grads, doc_lengths, in_proj, out_proj, in_factor, out_factor, index_rows)
     return scores.T
@@ -310,7 +331,7 @@
         in_proj.shape[1] % (16 * n) == 0
         and index_rows.shape[0] % (128 * n) == 0
         and tok % 16 == 0
-        and width % 256 == 0
+        and width % (128 * CHAINS) == 0
         and index_rows.shape[1] == in_proj.shape[1] ** 2 // n
         and (docs * sizes[2]) % 8 == 0
         and docs >= 2

time: 45.7 us -> 44.8 us (0.980)
  local copies, waits for them, and re-layouts: 3.15 us -> 1.28 us
  Pallas kernels: 42.4 us -> 43.3 us
    unnamed x7 -> x1, local copies, waits for them, and re-layouts: 3.15 us -> 1.28 us
    pallas_call x1, Pallas kernels: 42.4 us -> 43.3 us  [fused(): pl.pallas_call(functools.partial(kernel, sizes), out_shape=jax.ShapeDtype...]
where the time goes in v3:
time: 44.8 us; the launch traced here: 44.6 us
  Pallas kernels  43.3 us (97%)
  local copies, waits for them, and re-layouts  1.28 us (3%)
    pallas_call x1, Pallas kernels, fused(): pl.pallas_call(functools.partial(kernel, sizes), out_shape=jax.ShapeDtype...  43.3 us
    unnamed x1, local copies, waits for them, and re-layouts  1.28 us

profile of v3, /device:TPU:0, one launch (start us, length us, event | category | flops | bytes accessed | tf_op | source)
XLA Modules:
  0.0 44.6 jit_solution(18269524988220319139)
XLA Ops:
  0.0 43.3 %shard_map.82 = f32[8,128]{1,0:T(8,128)} custom-call(bf16[4,512,4096]{2,1,0:T(8,128)(2,1)} %x_hbm.1, bf16[4,512,4096]{2,1,0:T(8,128)(2,1)} %g_hbm.1, s32[4]{0:T(128)} %len_hbm.1, bf16[4096,256]{1,0:T(8,128)(2,1)} %wi_hbm.1, bf16[4096,256]{1,0:T(8,128)(2,1)} %wo_hbm.1, f32[256,256]{1,0:T(8,128)} %fi_hbm.1, f32[256,256]{1,0:T(8,128)} %fo_hbm.1, ...), custom_call_target="tpu_custom_call" | custom-call | tf_op jit(solution)/shard_map/pallas_call | solution.py:272
  43.3 1.3 %copy.10 = f32[128,8]{0,1:T(8,128)} copy(f32[128,8]{0,1:T(8,128)} %bitcast.1) | data formatting | bytes 8192

commit v4 on v3

--- a/solution.py
+++ b/solution.py
@@ -40,8 +40,8 @@
     sizes,
     x_hbm, g_hbm, len_hbm, wi_hbm, wo_hbm, fi_hbm, fo_hbm, idx_hbm,
     out_ref,
-    xbuf, idxbuf, wi, wo, fi, fo, lens, in_rows, out_rows, turned, send, recv, summed, sc_send, sc_recv,
-    piece_sem, idx_sem, weight_sem, send_sem, recv_sem, sc_send_sem, sc_recv_sem,
+    xbuf, idxbuf, wi, wo, fi, fo, lens, in_rows, out_rows, turned, part_sums, pair_send, pair_recv, send, recv, summed, sc_send, sc_recv,
+    piece_sem, idx_sem, weight_sem, pair_send_sem, pair_recv_sem, send_sem, recv_sem, sc_send_sem, sc_recv_sem,
 ):
     n_seq, n_sub, n_rep = sizes
     n = n_seq * n_sub * n_rep
@@ -51,8 +51,10 @@
     blocks = n // n_rep
     rows = idx_hbm.shape[0] // blocks
     lanes = rows // n_rep
-    place = lax.axis_index("seq") * n_sub + lax.axis_index("sub")
-    my_rep = lax.axis_index("rep")
+    my_seq, my_sub, my_rep = (lax.axis_index(axis) for axis in OWNERS)
+    place = my_seq * n_sub + my_sub
+    column = n_seq * n_rep
+    mine = my_seq * n_rep + my_rep
     me = place * n_rep + my_rep
 
     def device(p):
@@ -82,15 +84,40 @@
         source, target = ((wi_hbm, wi), (wo_hbm, wo), (fo_hbm, fo), (fi_hbm, fi), (len_hbm, lens))[k]
         return pltpu.make_async_copy(source, target, weight_sem.at[k])
 
-    def doc_copy(d, source, p):
+    def pair_copy(d, k):
+        to = lax.rem(my_sub + k, n_sub)
         return pltpu.make_async_remote_copy(
-            src_ref=send.at[d, p],
+            src_ref=pair_send.at[d, to],
+            dst_ref=pair_recv.at[d, k - 1],
+            send_sem=pair_send_sem.at[d, k - 1],
+            recv_sem=pair_recv_sem.at[d, k - 1],
+            device_id={"seq": my_seq, "sub": to, "rep": my_rep},
+            device_id_type=MESH,
+        )
+
+    def doc_copy(d, source, v):
+        return pltpu.make_async_remote_copy(
+            src_ref=send.at[d, v],
             dst_ref=recv.at[source, d],
-            send_sem=send_sem.at[d, p],
+            send_sem=send_sem.at[d, v],
             recv_sem=recv_sem.at[source, d],
-            device_id=device(p),
+            device_id={"seq": lax.div(v, n_rep), "sub": my_sub, "rep": lax.rem(v, n_rep)},
             device_id_type=MESH,
         )
+
+    def pass_on(d):
+        total = part_sums[my_sub]
+        for k in range(1, n_sub):
+            pair_copy(d, k).wait_recv()
+            total = total + pair_recv[d, k - 1].astype(F32)
+        send[d] = total.astype(BF16).reshape(send.shape[1:])
+
+        def push(s, c):
+            doc_copy(d, mine, lax.rem(mine + s, column)).start()
+            return c
+
+        lax.fori_loop(1, column, push, 0)
+        recv[mine, d] = send[d, mine]
 
     def score_copy(source, p):
         return pltpu.make_async_remote_copy(
@@ -149,6 +176,15 @@
             product = added(chains)
             if q == 0:
                 in_rows[...] = product.astype(BF16)
+
+                @pl.when(d == 0)
+                def _():
+                    pl.semaphore_wait(barrier, n - 1)
+
+                @pl.when(d > 0)
+                def _():
+                    pass_on(d - 1)
+
             else:
                 position = place * tok + lax.broadcasted_iota(jnp.int32, product.shape, 0)
                 out_rows[...] = jnp.where(position < lens[d], product, 0.0).astype(BF16)
@@ -172,43 +208,38 @@
             weight_copy(2).wait()
             weight_copy(3).wait()
 
-        left = dot3(fo[...], grad)
-        send[d] = left.astype(BF16).reshape(send.shape[1:])
-
-        @pl.when(d == 0)
-        def _():
-            pl.semaphore_wait(barrier, n - 1)
-
-        def push(s, c):
-            doc_copy(d, me, lax.rem(me + s, n)).start()
+        left = dot3(fo[...], grad).reshape(n_seq, n_sub, -1, grad.shape[1])
+        for k in range(n_sub):
+            part_sums[k] = left[:, k]
+            pair_send[d, k] = left[:, k].astype(BF16)
+
+        for k in range(1, n_sub):
+            pair_copy(d, k).start()
+        return carry
+
+    lax.fori_loop(0, docs, document, 0)
+    pass_on(docs - 1)
+
+    for d in range(docs):
+
+        def arrive(s, c):
+            doc_copy(d, lax.rem(mine + column - s, column), lax.rem(mine + s, column)).wait_recv()
             return c
 
-        lax.fori_loop(1, n, push, 0)
-        recv[me, d] = send[d, me]
-        return carry
-
-    lax.fori_loop(0, docs, document, 0)
-
-    for d in range(docs):
-
-        def arrive(s, c):
-            doc_copy(d, lax.rem(me + n - s, n), lax.rem(me + s, n)).wait_recv()
-            return c
-
-        lax.fori_loop(1, n, arrive, 0)
+        lax.fori_loop(1, column, arrive, 0)
         for r in range(n_rep):
             total = recv[r, d].astype(F32)
-            for j in range(1, blocks):
+            for j in range(1, n_seq):
                 total = total + recv[j * n_rep + r, d].astype(F32)
             summed[:, r * docs + d, :] = total
 
     o_rows, all_docs, rank = summed.shape
     columns = o_rows * all_docs
     precond = dot3(summed[...].reshape(columns, rank), fi[...]).T
-    column = lax.broadcasted_iota(jnp.int32, precond.shape, 1)
+    lane = lax.broadcasted_iota(jnp.int32, precond.shape, 1)
     for o in range(o_rows):
-        mine = (column >= o * all_docs) & (column < (o + 1) * all_docs)
-        turned[o] = jnp.where(mine, precond, 0.0).astype(BF16)
+        kept = (lane >= o * all_docs) & (lane < (o + 1) * all_docs)
+        turned[o] = jnp.where(kept, precond, 0.0).astype(BF16)
 
     def score(u, carry):
         for k in range(n_sub):
@@ -251,17 +282,24 @@
     out_ref[...] = jnp.sum(sc_recv[...], axis=0)
 
     def drain(s, carry):
-        p = lax.rem(me + s, n)
-        score_copy(me, p).wait_send()
-        for d in range(docs):
-            doc_copy(d, me, p).wait_send()
+        score_copy(me, lax.rem(me + s, n)).wait_send()
         return carry
 
     lax.fori_loop(1, n, drain, 0)
 
+    def drain_docs(d, carry):
+        for k in range(1, n_sub):
+            pair_copy(d, k).wait_send()
+        for s in range(1, column):
+            doc_copy(d, mine, lax.rem(mine + s, column)).wait_send()
+        return carry
+
+    lax.fori_loop(0, docs, drain_docs, 0)
+
 
 def fused(sizes, inputs, out_grads, doc_lengths, in_proj, out_proj, in_factor, out_factor, index_rows):
-    n = sizes[0] * sizes[1] * sizes[2]
+    n_seq, n_sub, n_rep = sizes
+    n = n_seq * n_sub * n_rep
     docs, tok, width = inputs.shape
     rank = in_proj.shape[1]
     rows, features = index_rows.shape
@@ -285,16 +323,21 @@
             pltpu.VMEM((tok, rank), BF16),
             pltpu.VMEM((tok, rank), BF16),
             pltpu.VMEM((o_rows, rank, o_rows * all_docs), BF16),
-            pltpu.VMEM((docs, n, o_rows, rank), BF16),
-            pltpu.VMEM((n, docs, o_rows, rank), BF16),
+            pltpu.VMEM((n_sub, n_seq, n_rep * o_rows, rank), F32),
+            pltpu.VMEM((docs, n_sub, n_seq, n_rep * o_rows, rank), BF16),
+            pltpu.VMEM((docs, n_sub - 1, n_seq, n_rep * o_rows, rank), BF16),
+            pltpu.VMEM((docs, n_seq * n_rep, o_rows, rank), BF16),
+            pltpu.VMEM((n_seq * n_rep, docs, o_rows, rank), BF16),
             pltpu.VMEM((o_rows, all_docs, rank), F32),
             pltpu.VMEM((n, all_docs, rows // n), F32),
             pltpu.VMEM((n, all_docs, rows // n), F32),
             pltpu.SemaphoreType.DMA((SLOTS,)),
             pltpu.SemaphoreType.DMA((blocks,)),
             pltpu.SemaphoreType.DMA((5,)),
-            pltpu.SemaphoreType.DMA((docs, n)),
-            pltpu.SemaphoreType.DMA((n, docs)),
+            pltpu.SemaphoreType.DMA((docs, n_sub - 1)),
+            pltpu.SemaphoreType.DMA((docs, n_sub - 1)),
+            pltpu.SemaphoreType.DMA((docs, n_seq * n_rep)),
+            pltpu.SemaphoreType.DMA((n_seq * n_rep, docs)),
             pltpu.SemaphoreType.DMA((n,)),
             pltpu.SemaphoreType.DMA((n,)),
         ],
@@ -335,6 +378,7 @@
         and index_rows.shape[1] == in_proj.shape[1] ** 2 // n
         and (docs * sizes[2]) % 8 == 0
         and docs >= 2
+        and sizes[1] >= 2
         and blocks == 2 * PIECES
     )
     return (fused if whole else general)(sizes, *arrays)

time: 44.8 us -> 49.7 us (1.11)
  Pallas kernels: 43.3 us -> 48.2 us
    pallas_call x1, Pallas kernels: 43.3 us -> 48.2 us  [fused(): pl.pallas_call(functools.partial(kernel, sizes), out_shape=jax.ShapeDtype...]
where the time goes in v4:
time: 49.7 us; the launch traced here: 49.5 us
  Pallas kernels  48.2 us (97%)
  local copies, waits for them, and re-layouts  1.28 us (3%)
    pallas_call x1, Pallas kernels, fused(): pl.pallas_call(functools.partial(kernel, sizes), out_shape=jax.ShapeDtype...  48.2 us
    unnamed x1, local copies, waits for them, and re-layouts  1.28 us

profile of v4, /device:TPU:0, one launch (start us, length us, event | category | flops | bytes accessed | tf_op | source)
XLA Modules:
  0.0 49.5 jit_solution(8598686068893845227)
XLA Ops:
  0.0 48.2 %shard_map.82 = f32[8,128]{1,0:T(8,128)} custom-call(bf16[4,512,4096]{2,1,0:T(8,128)(2,1)} %x_hbm.1, bf16[4,512,4096]{2,1,0:T(8,128)(2,1)} %g_hbm.1, s32[4]{0:T(128)} %len_hbm.1, bf16[4096,256]{1,0:T(8,128)(2,1)} %wi_hbm.1, bf16[4096,256]{1,0:T(8,128)(2,1)} %wo_hbm.1, f32[256,256]{1,0:T(8,128)} %fi_hbm.1, f32[256,256]{1,0:T(8,128)} %fo_hbm.1, ...), custom_call_target="tpu_custom_call" | custom-call | tf_op jit(solution)/shard_map/pallas_call | solution.py:310
  48.3 1.3 %copy.10 = f32[128,8]{0,1:T(8,128)} copy(f32[128,8]{0,1:T(8,128)} %bitcast.1) | data formatting | bytes 8192

commit v5 on v3

--- a/solution.py
+++ b/solution.py
@@ -40,7 +40,7 @@
     sizes,
     x_hbm, g_hbm, len_hbm, wi_hbm, wo_hbm, fi_hbm, fo_hbm, idx_hbm,
     out_ref,
-    xbuf, idxbuf, wi, wo, fi, fo, lens, in_rows, out_rows, turned, send, recv, summed, sc_send, sc_recv,
+    xbuf, idxbuf, wi, wo, fi, fo, lens, held, in_rows, out_rows, turned, send, recv, summed, sc_send, sc_recv,
     piece_sem, idx_sem, weight_sem, send_sem, recv_sem, sc_send_sem, sc_recv_sem,
 ):
     n_seq, n_sub, n_rep = sizes
@@ -51,16 +51,16 @@
     blocks = n // n_rep
     rows = idx_hbm.shape[0] // blocks
     lanes = rows // n_rep
-    place = lax.axis_index("seq") * n_sub + lax.axis_index("sub")
-    my_rep = lax.axis_index("rep")
+    my_seq, my_sub, my_rep = (lax.axis_index(axis) for axis in OWNERS)
+    place = my_seq * n_sub + my_sub
     me = place * n_rep + my_rep
 
-    def device(p):
-        return {
-            "seq": lax.div(p, n_sub * n_rep),
-            "sub": lax.rem(lax.div(p, n_rep), n_sub),
-            "rep": lax.rem(p, n_rep),
-        }
+    def others():
+        for shift in range(1, n):
+            seq = lax.rem(my_seq + shift // (n_sub * n_rep), n_seq)
+            sub = lax.rem(my_sub + shift // n_rep % n_sub, n_sub)
+            rep = lax.rem(my_rep + shift % n_rep, n_rep)
+            yield {"seq": seq, "sub": sub, "rep": rep}, (seq * n_sub + sub) * n_rep + rep
 
     def piece_copy(d, q):
         source = x_hbm if q < 2 else g_hbm
@@ -79,89 +79,97 @@
         )
 
     def weight_copy(k):
-        source, target = ((wi_hbm, wi), (wo_hbm, wo), (fo_hbm, fo), (fi_hbm, fi), (len_hbm, lens))[k]
+        halves = pl.ds(0, half), pl.ds(half, half)
+        source, target = (
+            (wi_hbm.at[halves[0], :], wi.at[halves[0], :]),
+            (wi_hbm.at[halves[1], :], wi.at[halves[1], :]),
+            (wo_hbm.at[halves[0], :], wo.at[halves[0], :]),
+            (wo_hbm.at[halves[1], :], wo.at[halves[1], :]),
+            (len_hbm, lens),
+            (fo_hbm, fo),
+            (fi_hbm, fi),
+        )[k]
         return pltpu.make_async_copy(source, target, weight_sem.at[k])
 
-    def doc_copy(d, source, p):
+    def doc_copy(d, source, p, target, count=None):
+        at = (lambda k: k) if count is None else (lambda k: pl.ds(k, count))
         return pltpu.make_async_remote_copy(
-            src_ref=send.at[d, p],
-            dst_ref=recv.at[source, d],
-            send_sem=send_sem.at[d, p],
-            recv_sem=recv_sem.at[source, d],
-            device_id=device(p),
+            src_ref=send.at[d, at(p)],
+            dst_ref=recv.at[d, at(source)],
+            send_sem=send_sem.at[d],
+            recv_sem=recv_sem.at[d],
+            device_id=target,
             device_id_type=MESH,
         )
 
-    def score_copy(source, p):
+    def score_copy(source, p, target, count=None):
+        at = (lambda k: k) if count is None else (lambda k: pl.ds(k, count))
         return pltpu.make_async_remote_copy(
-            src_ref=sc_send.at[p],
-            dst_ref=sc_recv.at[source],
-            send_sem=sc_send_sem.at[p],
-            recv_sem=sc_recv_sem.at[source],
-            device_id=device(p),
+            src_ref=sc_send.at[at(p)],
+            dst_ref=sc_recv.at[at(source)],
+            send_sem=sc_send_sem,
+            recv_sem=sc_recv_sem,
+            device_id=target,
             device_id_type=MESH,
         )
 
-    weight_copy(0).start()
-    piece_copy(0, 0).start()
-    piece_copy(0, 1).start()
-    weight_copy(1).start()
-    piece_copy(0, 2).start()
-    piece_copy(0, 3).start()
-    weight_copy(2).start()
-    weight_copy(3).start()
-    weight_copy(4).start()
+    next_device = next(others())[0]
+
     for q in range(PIECES):
-        piece_copy(1, q).start()
+        weight_copy(q).start()
+        piece_copy(0, q).start()
+    for k in range(PIECES, 7):
+        weight_copy(k).start()
 
     barrier = pltpu.get_barrier_semaphore()
 
-    def greet(s, carry):
-        p = lax.rem(me + s, n)
-        pl.semaphore_signal(barrier, inc=1, device_id=device(p), device_id_type=MESH)
-        return carry
-
-    lax.fori_loop(1, n, greet, 0)
+    for target, _ in others():
+        pl.semaphore_signal(barrier, inc=1, device_id=target, device_id_type=MESH)
 
     def document(d, carry):
         first = lax.rem(d, SLOTS // PIECES) * PIECES
-        for q in range(0, PIECES, 2):
+        for q in range(PIECES):
             piece_copy(d, q).wait()
-            piece_copy(d, q + 1).wait()
 
             @pl.when(d == 0)
             def _():
-                weight_copy(q // 2).wait()
-                if q == 2:
-                    weight_copy(4).wait()
-
-            w = wi if q == 0 else wo
+                weight_copy(q).wait()
+
+            @pl.when(d + 1 < docs)
+            def _():
+                piece_copy(d + 1, q).start()
+
+            @pl.when(d + 1 == docs)
+            def _():
+                idx_copy(q).start()
+                idx_copy(PIECES + q).start()
+
+            w = wi if q < 2 else wo
             chains = []
-            for k in range(CHAINS):
-                h, at = (k * 2) // CHAINS, (k % (CHAINS // 2)) * step
+            for k in range(CHAINS // 2):
+                row = (q % 2) * half + k * step
                 chains.append(
                     jnp.dot(
-                        xbuf[first + q + h, :, at : at + step],
-                        w[k * step : (k + 1) * step, :],
+                        xbuf[first + q, :, k * step : (k + 1) * step],
+                        w[row : row + step, :],
                         preferred_element_type=F32,
                     )
                 )
             product = added(chains)
-            if q == 0:
+            if q % 2 == 0:
+                held[...] = product
+            else:
+                product = held[...] + product
+            if q == 1:
                 in_rows[...] = product.astype(BF16)
-            else:
+            elif q == 3:
+
+                @pl.when(d == 0)
+                def _():
+                    weight_copy(4).wait()
+
                 position = place * tok + lax.broadcasted_iota(jnp.int32, product.shape, 0)
                 out_rows[...] = jnp.where(position < lens[d], product, 0.0).astype(BF16)
-            ahead = d + SLOTS // PIECES
-            for k in (q, q + 1):
-
-                @pl.when(ahead < docs)
-                def _():
-                    piece_copy(ahead, k).start()
-
-                @pl.when(ahead >= docs)
-                def _():
-                    idx_copy((ahead - docs) * PIECES + k).start()
 
         grad = lax.dot_general(
             out_rows[...], in_rows[...], (((0,), (0,)), ((), ())), preferred_element_type=F32
@@ -169,8 +177,8 @@
 
         @pl.when(d == 0)
         def _():
-            weight_copy(2).wait()
-            weight_copy(3).wait()
+            weight_copy(5).wait()
+            weight_copy(6).wait()
 
         left = dot3(fo[...], grad)
         send[d] = left.astype(BF16).reshape(send.shape[1:])
@@ -179,27 +187,19 @@
         def _():
             pl.semaphore_wait(barrier, n - 1)
 
-        def push(s, c):
-            doc_copy(d, me, lax.rem(me + s, n)).start()
-            return c
-
-        lax.fori_loop(1, n, push, 0)
-        recv[me, d] = send[d, me]
+        for target, p in others():
+            doc_copy(d, me, p, target).start()
+        recv[d, me] = send[d, me]
         return carry
 
     lax.fori_loop(0, docs, document, 0)
 
     for d in range(docs):
-
-        def arrive(s, c):
-            doc_copy(d, lax.rem(me + n - s, n), lax.rem(me + s, n)).wait_recv()
-            return c
-
-        lax.fori_loop(1, n, arrive, 0)
+        doc_copy(d, 0, 0, next_device, n - 1).wait_recv()
         for r in range(n_rep):
-            total = recv[r, d].astype(F32)
+            total = recv[d, r].astype(F32)
             for j in range(1, blocks):
-                total = total + recv[j * n_rep + r, d].astype(F32)
+                total = total + recv[d, j * n_rep + r].astype(F32)
             summed[:, r * docs + d, :] = total
 
     o_rows, all_docs, rank = summed.shape
@@ -235,29 +235,19 @@
 
                 @pl.when(p != me)
                 def _():
-                    score_copy(me, p).start()
+                    target = {"seq": lax.div(c, n_sub), "sub": lax.rem(c, n_sub), "rep": r}
+                    score_copy(me, p, target).start()
 
         return carry
 
     lax.fori_loop(0, n_seq, score, 0)
     sc_recv[me] = sc_send[me]
 
-    def settle(s, carry):
-        p = lax.rem(me + s, n)
-        score_copy(lax.rem(me + n - s, n), p).wait_recv()
-        return carry
-
-    lax.fori_loop(1, n, settle, 0)
+    score_copy(0, 0, next_device, n - 1).wait_recv()
     out_ref[...] = jnp.sum(sc_recv[...], axis=0)
-
-    def drain(s, carry):
-        p = lax.rem(me + s, n)
-        score_copy(me, p).wait_send()
-        for d in range(docs):
-            doc_copy(d, me, p).wait_send()
-        return carry
-
-    lax.fori_loop(1, n, drain, 0)
+    score_copy(0, 0, next_device, n - 1).wait_send()
+    for d in range(docs):
+        doc_copy(d, 0, 0, next_device, n - 1).wait_send()
 
 
 def fused(sizes, inputs, out_grads, doc_lengths, in_proj, out_proj, in_factor, out_factor, index_rows):
@@ -282,21 +272,22 @@
             pltpu.VMEM(in_factor.shape, F32),
             pltpu.VMEM(out_factor.shape, F32),
             pltpu.SMEM((docs,), jnp.int32),
+            pltpu.VMEM((tok, rank), F32),
             pltpu.VMEM((tok, rank), BF16),
             pltpu.VMEM((tok, rank), BF16),
             pltpu.VMEM((o_rows, rank, o_rows * all_docs), BF16),
             pltpu.VMEM((docs, n, o_rows, rank), BF16),
-            pltpu.VMEM((n, docs, o_rows, rank), BF16),
+            pltpu.VMEM((docs, n, o_rows, rank), BF16),
             pltpu.VMEM((o_rows, all_docs, rank), F32),
             pltpu.VMEM((n, all_docs, rows // n), F32),
             pltpu.VMEM((n, all_docs, rows // n), F32),
             pltpu.SemaphoreType.DMA((SLOTS,)),
             pltpu.SemaphoreType.DMA((blocks,)),
-            pltpu.SemaphoreType.DMA((5,)),
-            pltpu.SemaphoreType.DMA((docs, n)),
-            pltpu.SemaphoreType.DMA((n, docs)),
-            pltpu.SemaphoreType.DMA((n,)),
-            pltpu.SemaphoreType.DMA((n,)),
+            pltpu.SemaphoreType.DMA((7,)),
+            pltpu.SemaphoreType.DMA((docs,)),
+            pltpu.SemaphoreType.DMA((docs,)),
+            pltpu.SemaphoreType.DMA,
+            pltpu.SemaphoreType.DMA,
         ],
         compiler_params=pltpu.CompilerParams(
             collective_id=0, has_side_effects=True, vmem_limit_bytes=64 * 1024 * 1024

time: 44.8 us -> 42.3 us (0.944)
  Pallas kernels: 43.3 us -> 40.9 us
    pallas_call x1, Pallas kernels: 43.3 us -> 40.9 us  [fused(): pl.pallas_call(functools.partial(kernel, sizes), out_shape=jax.ShapeDtype...]
where the time goes in v5:
time: 42.3 us; the launch traced here: 42.2 us
  Pallas kernels  40.9 us (97%)
  local copies, waits for them, and re-layouts  1.28 us (3%)
    pallas_call x1, Pallas kernels, fused(): pl.pallas_call(functools.partial(kernel, sizes), out_shape=jax.ShapeDtype...  40.9 us
    unnamed x1, local copies, waits for them, and re-layouts  1.28 us

profile of v5, /device:TPU:0, one launch (start us, length us, event | category | flops | bytes accessed | tf_op | source)
XLA Modules:
  0.0 42.2 jit_solution(16117396857947640347)
XLA Ops:
  0.0 40.9 %shard_map.82 = f32[8,128]{1,0:T(8,128)} custom-call(bf16[4,512,4096]{2,1,0:T(8,128)(2,1)} %x_hbm.1, bf16[4,512,4096]{2,1,0:T(8,128)(2,1)} %g_hbm.1, s32[4]{0:T(128)} %len_hbm.1, bf16[4096,256]{1,0:T(8,128)(2,1)} %wi_hbm.1, bf16[4096,256]{1,0:T(8,128)(2,1)} %wo_hbm.1, f32[256,256]{1,0:T(8,128)} %fi_hbm.1, f32[256,256]{1,0:T(8,128)} %fo_hbm.1, ...), custom_call_target="tpu_custom_call" | custom-call | tf_op jit(solution)/shard_map/pallas_call | solution.py:262
  40.9 1.3 %copy.10 = f32[128,8]{0,1:T(8,128)} copy(f32[128,8]{0,1:T(8,128)} %bitcast.1) | data formatting | bytes 8192

commit v6 on v5

--- a/solution.py
+++ b/solution.py
@@ -141,8 +141,8 @@
 
             @pl.when(d + 1 == docs)
             def _():
-                idx_copy(q).start()
-                idx_copy(PIECES + q).start()
+                idx_copy(2 * q).start()
+                idx_copy(2 * q + 1).start()
 
             w = wi if q < 2 else wo
             chains = []
@@ -210,13 +210,13 @@
         mine = (column >= o * all_docs) & (column < (o + 1) * all_docs)
         turned[o] = jnp.where(mine, precond, 0.0).astype(BF16)
 
-    def score(u, carry):
+    def products(u):
         for k in range(n_sub):
             idx_copy(u * n_sub + k).wait()
         parts = []
         for k in range(CHAINS):
             o, wide = k * (o_rows // CHAINS), o_rows // CHAINS
-            block = idxbuf[pl.ds(u * n_sub, n_sub), :, o * rank : (o + wide) * rank]
+            block = idxbuf[u * n_sub : (u + 1) * n_sub, :, o * rank : (o + wide) * rank]
             parts.append(
                 jnp.dot(
                     block.reshape(n_sub * rows, wide * rank),
@@ -224,23 +224,32 @@
                     preferred_element_type=F32,
                 )
             )
-        part = added(parts).T
-        part = jnp.sum(part.reshape(o_rows, all_docs, n_sub * rows), axis=0)
+        return added(parts)
+
+    def hand_out(u, part):
+        part = jnp.sum(part.T.reshape(o_rows, all_docs, n_sub * rows), axis=0)
         for k in range(n_sub):
-            c = block_at(u * n_sub + k)
+            t = u * n_sub + k
+            c = block_at(t)
+            for r in range(n_rep):
+                at = (k * n_rep + r) * lanes
+                sc_send[c * n_rep + r] = part[:, at : at + lanes]
             for r in range(n_rep):
                 p = c * n_rep + r
-                at = (k * n_rep + r) * lanes
-                sc_send[p] = part[:, at : at + lanes]
-
-                @pl.when(p != me)
-                def _():
-                    target = {"seq": lax.div(c, n_sub), "sub": lax.rem(c, n_sub), "rep": r}
-                    score_copy(me, p, target).start()
-
-        return carry
-
-    lax.fori_loop(0, n_seq, score, 0)
+                copy = score_copy(
+                    me, p, {"seq": lax.div(c, n_sub), "sub": lax.rem(c, n_sub), "rep": r}
+                )
+                if t < blocks - 1:
+                    copy.start()
+                else:
+                    pl.when(r != my_rep)(copy.start)
+
+    part = products(0)
+    for u in range(1, n_seq):
+        later = products(u)
+        hand_out(u - 1, part)
+        part = later
+    hand_out(n_seq - 1, part)
     sc_recv[me] = sc_send[me]
 
     score_copy(0, 0, next_device, n - 1).wait_recv()

time: 42.3 us -> 46.8 us (1.11)
  Pallas kernels: 40.9 us -> 45.4 us
    pallas_call x1, Pallas kernels: 40.9 us -> 45.4 us  [fused(): pl.pallas_call(functools.partial(kernel, sizes), out_shape=jax.ShapeDtype...]
where the time goes in v6:
time: 46.8 us; the launch traced here: 46.7 us
  Pallas kernels  45.4 us (97%)
  local copies, waits for them, and re-layouts  1.28 us (3%)
    pallas_call x1, Pallas kernels, fused(): pl.pallas_call(functools.partial(kernel, sizes), out_shape=jax.ShapeDtype...  45.4 us
    unnamed x1, local copies, waits for them, and re-layouts  1.28 us

profile of v6, /device:TPU:0, one launch (start us, length us, event | category | flops | bytes accessed | tf_op | source)
XLA Modules:
  0.0 46.7 jit_solution(16878386435975841206)
XLA Ops:
  0.0 45.4 %shard_map.82 = f32[8,128]{1,0:T(8,128)} custom-call(bf16[4,512,4096]{2,1,0:T(8,128)(2,1)} %x_hbm.1, bf16[4,512,4096]{2,1,0:T(8,128)(2,1)} %g_hbm.1, s32[4]{0:T(128)} %len_hbm.1, bf16[4096,256]{1,0:T(8,128)(2,1)} %wi_hbm.1, bf16[4096,256]{1,0:T(8,128)(2,1)} %wo_hbm.1, f32[256,256]{1,0:T(8,128)} %fi_hbm.1, f32[256,256]{1,0:T(8,128)} %fo_hbm.1, ...), custom_call_target="tpu_custom_call" | custom-call | tf_op jit(solution)/shard_map/pallas_call | solution.py:271
  45.4 1.3 %copy.10 = f32[128,8]{0,1:T(8,128)} copy(f32[128,8]{0,1:T(8,128)} %bitcast.1) | data formatting | bytes 8192

commit v7 on v5

--- a/solution.py
+++ b/solution.py
@@ -40,7 +40,7 @@
     sizes,
     x_hbm, g_hbm, len_hbm, wi_hbm, wo_hbm, fi_hbm, fo_hbm, idx_hbm,
     out_ref,
-    xbuf, idxbuf, wi, wo, fi, fo, lens, held, in_rows, out_rows, turned, send, recv, summed, sc_send, sc_recv,
+    xbuf, idxbuf, weights, fi, fo, lens, held, in_rows, out_rows, turned, send, recv, summed, sc_send, sc_recv,
     piece_sem, idx_sem, weight_sem, send_sem, recv_sem, sc_send_sem, sc_recv_sem,
 ):
     n_seq, n_sub, n_rep = sizes
@@ -81,10 +81,10 @@
     def weight_copy(k):
         halves = pl.ds(0, half), pl.ds(half, half)
         source, target = (
-            (wi_hbm.at[halves[0], :], wi.at[halves[0], :]),
-            (wi_hbm.at[halves[1], :], wi.at[halves[1], :]),
-            (wo_hbm.at[halves[0], :], wo.at[halves[0], :]),
-            (wo_hbm.at[halves[1], :], wo.at[halves[1], :]),
+            (wi_hbm.at[halves[0], :], weights.at[0]),
+            (wi_hbm.at[halves[1], :], weights.at[1]),
+            (wo_hbm.at[halves[0], :], weights.at[2]),
+            (wo_hbm.at[halves[1], :], weights.at[3]),
             (len_hbm, lens),
             (fo_hbm, fo),
             (fi_hbm, fi),
@@ -128,49 +128,60 @@
 
     def document(d, carry):
         first = lax.rem(d, SLOTS // PIECES) * PIECES
-        for q in range(PIECES):
-            piece_copy(d, q).wait()
+        def piece(q, c):
+            slot = first + q
+            pltpu.make_async_copy(
+                x_hbm.at[d, :, pl.ds(0, half)], xbuf.at[slot], piece_sem.at[slot]
+            ).wait()
 
             @pl.when(d == 0)
             def _():
-                weight_copy(q).wait()
-
-            @pl.when(d + 1 < docs)
-            def _():
-                piece_copy(d + 1, q).start()
+                pltpu.make_async_copy(
+                    wi_hbm.at[pl.ds(0, half), :], weights.at[q], weight_sem.at[q]
+                ).wait()
+
+            for k in range(PIECES):
+
+                @pl.when((d + 1 < docs) & (q == k))
+                def _():
+                    piece_copy(d + 1, k).start()
 
             @pl.when(d + 1 == docs)
             def _():
-                idx_copy(q).start()
-                idx_copy(PIECES + q).start()
-
-            w = wi if q < 2 else wo
+                idx_copy(2 * q).start()
+                idx_copy(2 * q + 1).start()
+
             chains = []
             for k in range(CHAINS // 2):
-                row = (q % 2) * half + k * step
                 chains.append(
                     jnp.dot(
-                        xbuf[first + q, :, k * step : (k + 1) * step],
-                        w[row : row + step, :],
+                        xbuf[slot, :, k * step : (k + 1) * step],
+                        weights[q, k * step : (k + 1) * step, :],
                         preferred_element_type=F32,
                     )
                 )
             product = added(chains)
-            if q % 2 == 0:
-                held[...] = product
-            else:
-                product = held[...] + product
-            if q == 1:
-                in_rows[...] = product.astype(BF16)
-            elif q == 3:
-
-                @pl.when(d == 0)
-                def _():
-                    weight_copy(4).wait()
-
-                position = place * tok + lax.broadcasted_iota(jnp.int32, product.shape, 0)
-                out_rows[...] = jnp.where(position < lens[d], product, 0.0).astype(BF16)
-
+            side = lax.div(q, 2)
+
+            @pl.when(lax.rem(q, 2) == 0)
+            def _():
+                held[side] = product
+
+            @pl.when(lax.rem(q, 2) == 1)
+            def _():
+                held[side] = held[side] + product
+
+            return c
+
+        lax.fori_loop(0, PIECES, piece, 0)
+
+        @pl.when(d == 0)
+        def _():
+            weight_copy(4).wait()
+
+        in_rows[...] = held[0].astype(BF16)
+        position = place * tok + lax.broadcasted_iota(jnp.int32, (tok, held.shape[2]), 0)
+        out_rows[...] = jnp.where(position < lens[d], held[1], 0.0).astype(BF16)
         grad = lax.dot_general(
             out_rows[...], in_rows[...], (((0,), (0,)), ((), ())), preferred_element_type=F32
         )
@@ -267,12 +278,11 @@
         scratch_shapes=[
             pltpu.VMEM((SLOTS, tok, width // 2), BF16),
             pltpu.VMEM((blocks, rows // blocks, features), BF16),
-            pltpu.VMEM(in_proj.shape, BF16),
-            pltpu.VMEM(out_proj.shape, BF16),
+            pltpu.VMEM((PIECES, width // 2, rank), BF16),
             pltpu.VMEM(in_factor.shape, F32),
             pltpu.VMEM(out_factor.shape, F32),
             pltpu.SMEM((docs,), jnp.int32),
-            pltpu.VMEM((tok, rank), F32),
+            pltpu.VMEM((2, tok, rank), F32),
             pltpu.VMEM((tok, rank), BF16),
             pltpu.VMEM((tok, rank), BF16),
             pltpu.VMEM((o_rows, rank, o_rows * all_docs), BF16),

time: 42.3 us -> 35.9 us (0.85)
  Pallas kernels: 40.9 us -> 34.5 us
    pallas_call x1, Pallas kernels: 40.9 us -> 34.5 us  [fused(): pl.pallas_call(functools.partial(kernel, sizes), out_shape=jax.ShapeDtype...]
where the time goes in v7:
time: 35.9 us; the launch traced here: 35.7 us
  Pallas kernels  34.5 us (96%)
  local copies, waits for them, and re-layouts  1.28 us (4%)
    pallas_call x1, Pallas kernels, fused(): pl.pallas_call(functools.partial(kernel, sizes), out_shape=jax.ShapeDtype...  34.5 us
    unnamed x1, local copies, waits for them, and re-layouts  1.28 us

profile of v7, /device:TPU:0, one launch (start us, length us, event | category | flops | bytes accessed | tf_op | source)
XLA Modules:
  0.0 35.7 jit_solution(10576412035640195340)
XLA Ops:
  0.0 34.5 %shard_map.82 = f32[8,128]{1,0:T(8,128)} custom-call(bf16[4,512,4096]{2,1,0:T(8,128)(2,1)} %x_hbm.1, bf16[4,512,4096]{2,1,0:T(8,128)(2,1)} %g_hbm.1, s32[4]{0:T(128)} %len_hbm.1, bf16[4096,256]{1,0:T(8,128)(2,1)} %wi_hbm.1, bf16[4096,256]{1,0:T(8,128)(2,1)} %wo_hbm.1, f32[256,256]{1,0:T(8,128)} %fi_hbm.1, f32[256,256]{1,0:T(8,128)} %fo_hbm.1, ...), custom_call_target="tpu_custom_call" | custom-call | tf_op jit(solution)/shard_map/pallas_call | solution.py:273
  34.5 1.3 %copy.10 = f32[128,8]{0,1:T(8,128)} copy(f32[128,8]{0,1:T(8,128)} %bitcast.1) | data formatting | bytes 8192
